TPU v7x, 512 devices: a whole 4x8x8 slice. The times are simulated.
512 devices in a mesh: row: 16 (over z_lo, x), col: 8 (over y), fiber: 4 (over z_hi, core).
Axes of the slice: x: 4, y: 8, z: 8 (z_hi: 2, z_lo: 4; z = z_hi * 4 + z_lo), core: 2. Of those that a mesh axis runs over, the one named last changes fastest.
Arguments:
- values: float32 [12288, 12288], P('row', ('col', 'fiber')), may hold values from -6 to 6
- tile_mask: int32 [96, 96], P('row', ('col', 'fiber')), may hold values from 0 to 1, as said below
- keep_mask: int32 [96, 96], P('row', ('col', 'fiber')), may hold values 0 or 1
Outputs:
- flows: float32 [12288, 12288], P('row', ('col', 'fiber'))
Inputs may be any that keep to these rules, and one draw needn't show every extreme that they name: `tile_mask`: 1 marks a tile that holds entries; every diagonal tile is 1, and tiles with low indices are denser.
All inputs are finite; a program needn't handle non-finite values. No bound on the sum of `keep_mask` on one device may be relied on, other than what follows from the above.
Results may differ from a plain program's by a relative error of at most 0.017.
Values may be sent and summed in bfloat16 or wider, within the bound.
No kernel may reach another device: no remote copies, remote signals or barrier semaphores. Data moves between devices by JAX's collectives and lax.ppermute only.
A program may use at most 64 MiB of HBM per device.

v0:
```python
import jax
import jax.numpy as jnp
from jax import lax
from jax.sharding import PartitionSpec as P


def cut_along(shard, dim, peers):
    lengths = shard.shape
    parts = shard.reshape(*lengths[:dim], peers, lengths[dim] // peers, *lengths[dim + 1 :])
    return jnp.moveaxis(parts, dim, 0)


def sum_at_owner(shard, axis, dim):
    parts = cut_along(shard, dim, lax.axis_size(axis))
    arrived = lax.all_to_all(parts, axis, split_axis=0, concat_axis=0, tiled=True)
    return arrived.astype(jnp.float32).sum(axis=0)


def sent_to_all(shard, axis):
    copies = jnp.broadcast_to(shard, (lax.axis_size(axis), *shard.shape))
    return lax.all_to_all(copies, axis, split_axis=0, concat_axis=0, tiled=True)


def taken_together(shard, axis):
    return sent_to_all(shard, axis).sum(axis=0)


def spread_tiles(mask, tile_size):
    count_rows, count_cols = mask.shape
    wide = jnp.broadcast_to(
        mask.astype(jnp.float32)[:, None, :, None], (count_rows, tile_size, count_cols, tile_size)
    )
    return wide.reshape(count_rows * tile_size, count_cols * tile_size)


def local(values, tile_mask, keep_mask):
    n_row = lax.axis_size("row")
    n_fib = lax.axis_size("fiber")
    tile_size = values.shape[1] // tile_mask.shape[1]
    weighted = (values * spread_tiles(tile_mask, tile_size)).astype(jnp.bfloat16)
    rows_dev, unit_width = weighted.shape
    sub_width = unit_width // n_fib
    unit_count = rows_dev // unit_width
    left_stack = weighted.reshape(rows_dev, n_fib, sub_width)
    right_stack = weighted.reshape(unit_count, n_fib, sub_width, unit_width)
    left_recv, right_recv = (
        lax.all_to_all(left_stack, "fiber", split_axis=1, concat_axis=1, tiled=True),
        lax.all_to_all(right_stack, "fiber", split_axis=1, concat_axis=1, tiled=True),
    )
    left_local = left_recv.reshape(rows_dev, unit_width)
    right_local = jnp.transpose(right_recv, (0, 2, 1, 3)).reshape(
        unit_count * sub_width, n_fib * unit_width
    )
    left_all = lax.all_gather(left_local, "col", axis=1, tiled=True)
    partial_product = jnp.dot(
        left_all,
        lax.all_gather(right_local, "row", axis=0, tiled=True),
        preferred_element_type=jnp.float32,
    )
    expanded = sum_at_owner(partial_product.astype(jnp.bfloat16), "fiber", 1)
    squared = expanded * expanded
    col_total = taken_together(jnp.sum(squared, axis=0), "row")
    col_scale = col_total / (rows_dev * n_row) + 1e-06
    return spread_tiles(keep_mask, tile_size) * squared / col_scale[None, :]


def solution(mesh):
    return jax.shard_map(
        local,
        mesh=mesh,
        in_specs=(
            P("row", ("col", "fiber")),
            P("row", ("col", "fiber")),
            P("row", ("col", "fiber")),
        ),
        out_specs=P("row", ("col", "fiber")),
        check_vma=False,
    )
```

profile of v0, /device:TPU:8, one launch (start us, length us, event | category | flops | bytes accessed | tf_op | source)
XLA Modules:
  0.0 311.7 jit_solution(8198016643156649648)
XLA Ops:
  6.5 0.0 all-gather.3.cloned.1.call-start
  6.5 0.7 convert_element_type.16
  7.2 1.6 copy.27
  8.9 0.2 broadcast_in_dim.7
  9.0 0.4 fusion
  9.4 30.0 %all_to_all.21 = bf16[768,4,96]{0,2,1:T(8,128)(2,1)} all-to-all(bf16[768,4,96]{0,2,1:T(8,128)(2,1)S(1)} %bitcast.34), channel_id=1, replica_groups=mesh['row'=16,'col'=8,'fiber'=4] {'fiber'}, dimensions={1} | all-to-all | bytes 1179648 | tf_op jit(solution)/shard_map/all_to_all | solution.py:47
  39.4 0.0 all-gather.3.cloned.1.call-update
  39.4 0.0 all-gather.5.cloned.1.call-start
  39.4 0.3 copy.28
  39.7 0.1 copy.29
  39.8 22.0 %all_to_all.22 = bf16[2,4,96,384]{3,2,0,1:T(8,128)(2,1)S(1)} all-to-all(bf16[2,4,96,384]{3,2,0,1:T(8,128)(2,1)S(1)} %copy.29), channel_id=1, replica_groups=mesh['row'=16,'col'=8,'fiber'=4] {'fiber'}, dimensions={1} | all-to-all | bytes 1179648 | tf_op jit(solution)/shard_map/all_to_all | solution.py:48
  61.9 0.5 copy.30
  62.3 0.9 copy.40
  63.2 0.0 all-gather.5.cloned.1.call-update
  63.2 34.8 %all-gather.3.cloned.1.call-done = bf16[768,3072]{0,1:T(8,128)(2,1)} async-done(((bf16[768,384]{0,1:T(8,128)(2,1)}), bf16[768,3072]{0,1:T(8,128)(2,1)}) %all-gather.3.cloned.1.call-update) | async-done | bytes 4718608 | tf_op jit(solution)/shard_map/all_gather | solution.py:54
  98.0 118.6 %all-gather.5.cloned.1.call-done = bf16[3072,1536]{1,0:T(8,128)(2,1)} async-done(((bf16[192,1536]{1,0:T(8,128)(2,1)}), bf16[3072,1536]{1,0:T(8,128)(2,1)}) %all-gather.5.cloned.1.call-update) | async-done | bytes 9437200 | tf_op jit(solution)/shard_map/all_gather | solution.py:57
  216.6 11.6 %convolution_convert_fusion = bf16[768,1536]{1,0:T(8,128)(2,1)S(1)} fusion(bf16[768,3072]{0,1:T(8,128)(2,1)} %all-gather.3.cloned.1.call-done, bf16[3072,1536]{1,0:T(8,128)(2,1)} %all-gather.5.cloned.1.call-done), kind=kOutput, calls=%fused_computation.1 | convolution fusion | flops 7248936960 | bytes 16515072 | tf_op jit(solution)/shard_map/dot_general | solution.py:55
  228.2 0.2 copy.44
  228.5 61.1 %all_to_all.23 = bf16[4,768,384]{2,1,0:T(8,128)(2,1)S(1)} all-to-all(bf16[4,768,384]{2,1,0:T(8,128)(2,1)S(1)} %bitcast.31), channel_id=1, replica_groups=mesh['row'=16,'col'=8,'fiber'=4] {'fiber'}, dimensions={0} | all-to-all | bytes 4718592 | tf_op jit(solution)/shard_map/all_to_all | solution.py:15
  289.6 0.0 copy-start
  289.6 0.4 convert_reduce_fusion
  289.9 0.1 multiply_reduce_fusion
  290.1 0.6 broadcast_in_dim.8
  290.7 4.1 %all-to-all-start.3 = ((f32[16,1,384]{2,1,0:T(1,128)}), f32[16,1,384]{2,1,0:T(1,128)}, u32[]{:S(2)}, u32[]{:S(2)}) async-start(f32[16,1,384]{2,1,0:T(1,128)} %broadcast_in_dim.8), calls=%async_computation.3 | async-start | bytes 49152 | tf_op jit(solution)/shard_map/all_to_all | solution.py:21
  294.8 0.0 copy-done
  294.9 0.2 broadcast_in_dim.6
  295.0 0.3 copy.45
  295.3 0.4 copy.33
  295.7 7.3 %all-to-all-done.3 = f32[16,1,384]{2,1,0:T(1,128)} async-done(((f32[16,1,384]{2,1,0:T(1,128)}), f32[16,1,384]{2,1,0:T(1,128)}, u32[]{:S(2)}, u32[]{:S(2)}) %all-to-all-start.3) | async-done | bytes 24608 | tf_op jit(solution)/shard_map/all_to_all | solution.py:21
  302.9 0.8 reduce_sum.29
  303.7 1.1 multiply_divide_fusion
  (2 shorter events, 0.0 us)
Async XLA Ops:
  6.5 91.5 %all-gather.3.cloned.1.call-start = ((), (), s32[]{:S(2)}) async-start(), calls=%async_computation.4 | async-start | bytes 5308416 | tf_op jit(solution)/shard_map/all_gather | solution.py:54
  39.4 177.2 %all-gather.5.cloned.1.call-start = ((), (), s32[]{:S(2)}) async-start(), calls=%async_computation.5 | async-start | bytes 10027008 | tf_op jit(solution)/shard_map/all_gather | solution.py:57
  289.6 5.3 %copy-start = (s32[6,3]{0,1:T(4,128)S(1)}, s32[6,3]{0,1:T(4,128)}, u32[]{:S(2)}) copy-start(s32[6,3]{0,1:T(4,128)} %param.5) | copy-start | bytes 220
  290.7 12.2 %all-to-all-start.3 = ((f32[16,1,384]{2,1,0:T(1,128)}), f32[16,1,384]{2,1,0:T(1,128)}, u32[]{:S(2)}, u32[]{:S(2)}) async-start(f32[16,1,384]{2,1,0:T(1,128)} %broadcast_in_dim.8), calls=%async_computation.3 | async-start | bytes 49152 | tf_op jit(solution)/shard_map/all_to_all | solution.py:21
Sparse Core Ops, SparseCore 0:
  39.5 58.4 all-gather.2
  100.1 116.4 all-gather.4
where the time goes:
time: 312 us
  waiting for transfers between devices  161 us (52%)
  blocking collectives  113 us (36%)
  between operations  13.5 us (4%)
  matrix products  11.6 us (4%)
  local copies, waits for them, and re-layouts  5.17 us (2%)
  starting transfers between devices  4.18 us (1%)
  other arithmetic  3.47 us (1%)
    all_gather x1, waiting for transfers between devices, local(): lax.all_gather(right_local, 'row', axis=0, tiled=True)  119 us
    all_to_all x1, blocking collectives, sum_at_owner(): lax.all_to_all(parts, axis, split_axis=0, concat_axis=0, tiled=True)  61.1 us
    all_gather x1, waiting for transfers between devices, local(): left_all = lax.all_gather(left_local, 'col', axis=1, tiled=True)  34.8 us
    all_to_all x1, blocking collectives, local(): lax.all_to_all(left_stack, 'fiber', split_axis=1, concat_axis=1, tiled=True)  30 us
    all_to_all x1, blocking collectives, local(): lax.all_to_all(right_stack, 'fiber', split_axis=1, concat_axis=1, tiled=T...  22 us
    dot_general x1, matrix products, local(): jnp.dot(left_all, lax.all_gather(right_local, 'row', axis=0, tiled=True),...  11.6 us
    all_to_all x1, waiting for transfers between devices, sent_to_all(): return lax.all_to_all(copies, axis, split_axis=0, concat_axis=0, tiled=True)  7.26 us
  transfers between devices with their start and end apart: 3, of which 3 were waited for; matrix products, arithmetic and copies ran while one was open for 1% of the time, Pallas kernels for 0%

commit v1 on v0

--- a/solution.py
+++ b/solution.py
@@ -51,7 +51,10 @@
     right_local = jnp.transpose(right_recv, (0, 2, 1, 3)).reshape(
         unit_count * sub_width, n_fib * unit_width
     )
-    left_all = lax.all_gather(left_local, "col", axis=1, tiled=True)
+    shares = lax.axis_size("col")
+    next_value = tuple((shares if t == 1 else 1 for t in range(left_local.ndim)))
+    local_part = jnp.tile(left_local, next_value)
+    left_all = lax.all_to_all(local_part, axis_name="col", split_axis=1, concat_axis=1, tiled=True)
     partial_product = jnp.dot(
         left_all,
         lax.all_gather(right_local, "row", axis=0, tiled=True),

time: 312 us -> 275 us (0.88)
  the two profiles are of different devices: /device:TPU:8 before, /device:TPU:1 now
where the time goes in v1:
time: 275 us; the launch traced here: 274 us
  blocking collectives  196 us (71%)
  starting transfers between devices  31.6 us (11%)
  between operations  13.5 us (5%)
  local copies, waits for them, and re-layouts  12.5 us (5%)
  matrix products  11.6 us (4%)
  waiting for transfers between devices  6.17 us (2%)
  other arithmetic  3.47 us (1%)
    all_to_all x1, blocking collectives, local(): lax.all_to_all(local_part, axis_name='col', split_axis=1, concat_axis=1,...  111 us
    all_to_all x1, blocking collectives, sum_at_owner(): lax.all_to_all(parts, axis, split_axis=0, concat_axis=0, tiled=True)  38.2 us
    all_to_all x1, starting transfers between devices, sent_to_all(): return lax.all_to_all(copies, axis, split_axis=0, concat_axis=0, tiled=True)  31.6 us
    all_to_all x1, blocking collectives, local(): lax.all_to_all(right_stack, 'fiber', split_axis=1, concat_axis=1, tiled=T...  24.4 us
    all_to_all x1, blocking collectives, local(): lax.all_to_all(left_stack, 'fiber', split_axis=1, concat_axis=1, tiled=True)  22.1 us
    dot_general x1, matrix products, local(): jnp.dot(left_all, lax.all_gather(right_local, 'row', axis=0, tiled=True),...  11.6 us
    all_to_all x1, local copies, waits for them, and re-layouts, local(): lax.all_to_all(local_part, axis_name='col', split_axis=1, concat_axis=1,...  6.63 us
    all_to_all x1, waiting for transfers between devices, sent_to_all(): return lax.all_to_all(copies, axis, split_axis=0, concat_axis=0, tiled=True)  6.15 us
  transfers between devices with their start and end apart: 2, of which 1 were waited for; matrix products, arithmetic and copies ran while one was open for 3% of the time, Pallas kernels for 0%

profile of v1, /device:TPU:1, one launch (start us, length us, event | category | flops | bytes accessed | tf_op | source)
XLA Modules:
  0.0 274.5 jit_solution(17442200153729818719)
XLA Ops:
  6.5 0.0 all-gather.2.cloned.1.call-start
  6.5 0.7 convert_element_type.16
  7.2 1.6 copy.41
  8.9 0.2 broadcast_in_dim.7
  9.0 0.4 fusion
  9.4 0.3 copy.44
  9.7 0.1 copy.45
  9.8 24.4 %all_to_all.30 = bf16[2,4,96,384]{3,2,0,1:T(8,128)(2,1)S(1)} all-to-all(bf16[2,4,96,384]{3,2,0,1:T(8,128)(2,1)S(1)} %copy.45), channel_id=1, replica_groups=mesh['row'=16,'col'=8,'fiber'=4] {'fiber'}, dimensions={1} | all-to-all | bytes 1179648 | tf_op jit(solution)/shard_map/all_to_all | solution.py:48
  34.2 0.5 copy.46
  34.7 0.9 copy.56
  35.6 0.0 all-gather.2.cloned.1.call-update
  35.6 22.1 %all_to_all.31 = bf16[768,4,96]{0,2,1:T(8,128)(2,1)S(1)} all-to-all(bf16[768,4,96]{0,2,1:T(8,128)(2,1)S(1)} %bitcast.35), channel_id=1, replica_groups=mesh['row'=16,'col'=8,'fiber'=4] {'fiber'}, dimensions={1} | all-to-all | bytes 1179648 | tf_op jit(solution)/shard_map/all_to_all | solution.py:47
  57.7 0.3 copy.42
  58.0 0.4 tile.9
  58.5 110.9 %all_to_all.32 = bf16[768,8,384]{2,0,1:T(8,128)(2,1)} all-to-all(bf16[768,8,384]{2,0,1:T(8,128)(2,1)S(1)} %tile.9), channel_id=1, replica_groups=mesh['row'=16,'col'=8,'fiber'=4] {'col'}, dimensions={1} | all-to-all | bytes 9437184 | tf_op jit(solution)/shard_map/all_to_all | solution.py:57
  169.4 6.6 %copy.43 = bf16[768,8,384]{0,2,1:T(8,128)(2,1)} copy(bf16[768,8,384]{2,0,1:T(8,128)(2,1)} %all_to_all.32) | data formatting | bytes 9437184 | tf_op jit(solution)/shard_map/all_to_all | solution.py:57
  176.0 0.0 all-gather.2.cloned.1.call-done
  176.0 11.6 %convolution_convert_fusion = bf16[768,1536]{1,0:T(8,128)(2,1)S(1)} fusion(bf16[768,3072]{0,1:T(8,128)(2,1)} %bitcast.36, bf16[3072,1536]{1,0:T(8,128)(2,1)} %all-gather.2.cloned.1.call-done), kind=kOutput, calls=%fused_computation.1 | convolution fusion | flops 7248936960 | bytes 16515072 | tf_op jit(solution)/shard_map/dot_general | solution.py:58
  187.6 0.2 copy.60
  187.9 38.2 %all_to_all.33 = bf16[4,768,384]{2,1,0:T(8,128)(2,1)S(1)} all-to-all(bf16[4,768,384]{2,1,0:T(8,128)(2,1)S(1)} %bitcast.32), channel_id=1, replica_groups=mesh['row'=16,'col'=8,'fiber'=4] {'fiber'}, dimensions={0} | all-to-all | bytes 4718592 | tf_op jit(solution)/shard_map/all_to_all | solution.py:15
  226.0 0.0 copy-start
  226.0 0.4 convert_reduce_fusion
  226.4 0.1 multiply_reduce_fusion
  226.5 0.6 broadcast_in_dim.8
  227.2 31.6 %all-to-all-start.4 = ((f32[16,1,384]{2,1,0:T(1,128)}), f32[16,1,384]{2,1,0:T(1,128)}, u32[]{:S(2)}, u32[]{:S(2)}) async-start(f32[16,1,384]{2,1,0:T(1,128)} %broadcast_in_dim.8), calls=%async_computation.4 | async-start | bytes 49152 | tf_op jit(solution)/shard_map/all_to_all | solution.py:21
  258.7 0.0 copy-done
  258.8 0.2 broadcast_in_dim.6
  258.9 0.3 copy.61
  259.2 0.4 copy.49
  259.6 6.2 %all-to-all-done.4 = f32[16,1,384]{2,1,0:T(1,128)} async-done(((f32[16,1,384]{2,1,0:T(1,128)}), f32[16,1,384]{2,1,0:T(1,128)}, u32[]{:S(2)}, u32[]{:S(2)}) %all-to-all-start.4) | async-done | bytes 24608 | tf_op jit(solution)/shard_map/all_to_all | solution.py:21
  265.7 0.8 reduce_sum.29
  266.5 1.1 multiply_divide_fusion
  (2 shorter events, 0.0 us)
Async XLA Ops:
  6.5 169.5 %all-gather.2.cloned.1.call-start = ((), (), s32[]{:S(2)}) async-start(), calls=%async_computation.5 | async-start | bytes 10027008 | tf_op jit(solution)/shard_map/all_gather | solution.py:60
  226.0 32.7 %copy-start = (s32[6,3]{0,1:T(4,128)S(1)}, s32[6,3]{0,1:T(4,128)}, u32[]{:S(2)}) copy-start(s32[6,3]{0,1:T(4,128)} %param.5) | copy-start | bytes 220
  227.2 38.6 %all-to-all-start.4 = ((f32[16,1,384]{2,1,0:T(1,128)}), f32[16,1,384]{2,1,0:T(1,128)}, u32[]{:S(2)}, u32[]{:S(2)}) async-start(f32[16,1,384]{2,1,0:T(1,128)} %broadcast_in_dim.8), calls=%async_computation.4 | async-start | bytes 49152 | tf_op jit(solution)/shard_map/all_to_all | solution.py:21
Sparse Core Ops, SparseCore 0:
  35.7 126.3 all-gather.1
